TPU v7x, 256 devices: a whole 4x4x8 slice. The times are simulated.
256 devices in a mesh: section: 16 (over y, z_lo), dp: 16 (over x, z_hi, core).
Axes of the slice: x: 4, y: 4, z: 8 (z_hi: 2, z_lo: 4; z = z_hi * 4 + z_lo), core: 2. Of those that a mesh axis runs over, the one named last changes fastest.
Arguments:
- latents: bfloat16 [2, 16, 8, 8, 640], P(None, 'dp'), may hold values from -6 to 6
- cotangent: bfloat16 [2, 16, 8, 8, 640], P(None, 'dp'), may hold values from -6 to 6
- conv_weight: bfloat16 [16, 3, 3, 640, 640], P('section'), may hold values from -0.078125 to 0.078125
- timesteps: int32 [2, 16], P(None, 'dp'), may hold values from 0 to 999
- time_table: float32 [1000, 640], replicated, may hold values from -6 to 6
Outputs:
- weight_grads: float32 [16, 3, 3, 640, 640], P('section', None, None, None, 'dp')
All inputs are finite; a program needn't handle non-finite values.
Results may differ from a plain program's by a relative error of at most 0.027.
Values may be sent and summed in bfloat16 or wider, within the bound.
A program may use at most 128 MiB of HBM per device.

v0:
```python
import math

import jax
import jax.numpy as jnp
from jax import lax
from jax.sharding import PartitionSpec as P

EPS = 1e-05


def from_partner(block, axis, distance):
    count = lax.axis_size(axis)
    route = []
    for low in range(count):
        high = low | 1 << distance
        if high != low and high < count:
            route += [(low, high), (high, low)]
    return lax.ppermute(block, axis, route)


def shifted(x, axis, by):
    size = lax.axis_size(axis)
    pairs = [(i, i + by) for i in range(size) if 0 <= i + by < size]
    return lax.ppermute(x, axis, pairs)


def normalize(inputs):
    inv_rms = lax.rsqrt(jnp.mean(inputs * inputs, axis=-1, keepdims=True) + EPS)
    return (inv_rms, inputs * inv_rms)


def conv_forward(normed_b, weight):
    return lax.conv_general_dilated(
        normed_b,
        weight,
        (1, 1),
        "SAME",
        dimension_numbers=("NHWC", "HWIO", "NHWC"),
        preferred_element_type=jnp.float32,
    )


def conv_input_grad(grad_b, weight):
    flipped = weight[::-1, ::-1]
    return lax.conv_general_dilated(
        grad_b,
        flipped,
        (1, 1),
        "SAME",
        dimension_numbers=("NHWC", "HWOI", "NHWC"),
        preferred_element_type=jnp.float32,
    )


def conv_weight_grad(normed_b, grad_b):
    side_h, side_w = (normed_b.shape[1], normed_b.shape[2])
    padded = jnp.pad(normed_b, ((0, 0), (1, 1), (1, 1), (0, 0)))
    kernel_rows = []
    for shift_h in range(3):
        kernel_cols = []
        for shift_w in range(3):
            window = padded[:, shift_h : shift_h + side_h, shift_w : shift_w + side_w, :]
            kernel_cols.append(
                jnp.einsum("bhwi,bhwo->io", window, grad_b, preferred_element_type=jnp.float32)
            )
        kernel_rows.append(jnp.stack(kernel_cols))
    return jnp.stack(kernel_rows)


def stored_weight_grad(normed_store, gpre_store):
    merged = (-1,) + normed_store.shape[2:]
    return conv_weight_grad(normed_store.reshape(merged), gpre_store.reshape(merged))


def level_forward(inputs, weight, t_embed):
    inv_rms, normed = normalize(inputs)
    pre_act = conv_forward(normed.astype(jnp.bfloat16), weight) + t_embed[:, None, None, :]
    branch = pre_act * jax.nn.sigmoid(pre_act)
    return ((inputs + branch).astype(jnp.bfloat16), branch.astype(jnp.bfloat16), pre_act)


def level_backward(inputs, weight, pre_act, grad_out, grad_branch):
    inv_rms, normed = normalize(inputs)
    normed_b = normed.astype(jnp.bfloat16)
    sigmoid_pre = jax.nn.sigmoid(pre_act)
    grad_pre = (grad_branch * sigmoid_pre * (1.0 + pre_act * (1.0 - sigmoid_pre))).astype(
        jnp.bfloat16
    )
    grad_normed = conv_input_grad(grad_pre, weight)
    grad_in = grad_out + inv_rms * (
        grad_normed - normed * jnp.mean(grad_normed * normed, axis=-1, keepdims=True)
    )
    return (grad_in.astype(jnp.bfloat16), normed_b, grad_pre)


def mirror(fields):
    bit_count = lax.axis_size("section").bit_length() - 1
    bit_order = list(range(bit_count))
    for bit_index in bit_order:
        fields = from_partner(fields, "section", bit_index)
    return fields


def store_slot(buffer, update, slot_index, enabled):
    current = lax.dynamic_index_in_dim(buffer, slot_index, 0, keepdims=False)
    return lax.dynamic_update_index_in_dim(
        buffer, jnp.where(enabled, update, current), slot_index, 0
    )


def on_device(latents, cotangent, conv_weight, timesteps, time_table):
    section_count = lax.axis_size("section")
    half_count = section_count // 2
    section_index = lax.axis_index("section")
    micro_count = latents.shape[0]
    weight = conv_weight[0]
    table_ids = jnp.arange(time_table.shape[0], dtype=jnp.int32)
    onehot = (timesteps[:, :, None] == table_ids[None, None, :]).astype(jnp.float32)
    t_embed = jnp.einsum("msk,kc->msc", onehot, time_table, precision=lax.Precision.HIGHEST)
    zeros_acts = jnp.zeros_like(latents)
    zero_field = jnp.zeros(latents.shape[1:], jnp.bfloat16)
    zero_pre = jnp.zeros(latents.shape[1:], jnp.float32)
    tick_count = half_count + micro_count - 1

    def forward_phase(first_section, carried, skip_in):

        def forward_tick_body(tick_index, loop_state):
            inbox, pre_acts, branches = loop_state
            offset = section_index - first_section
            micro_index = tick_index - offset
            active = (
                (offset >= 0)
                & (offset < half_count)
                & (micro_index >= 0)
                & (micro_index < micro_count)
            )
            slot_index = jnp.clip(micro_index, 0, micro_count - 1)

            def forward_compute():
                inputs = inbox[slot_index].astype(jnp.float32) + skip_in[slot_index].astype(
                    jnp.float32
                )
                return level_forward(inputs, weight, t_embed[slot_index])

            def forward_nothing():
                return (zero_field, zero_field, zero_pre)

            outgoing, branch, pre_act = lax.cond(active, forward_compute, forward_nothing)
            received = shifted(outgoing, "section", 1)
            recv_slot = tick_index - offset + 1
            receives = (
                (offset >= 1)
                & (offset <= half_count)
                & (recv_slot >= 0)
                & (recv_slot < micro_count)
            )
            inbox = store_slot(inbox, received, jnp.clip(recv_slot, 0, micro_count - 1), receives)
            pre_acts = store_slot(pre_acts, pre_act, slot_index, active)
            branches = store_slot(branches, branch, slot_index, active)
            return (inbox, pre_acts, branches)

        return lax.fori_loop(0, tick_count, forward_tick_body, carried)

    inbox = jnp.where(section_index == 0, latents, zeros_acts)
    pre_acts = jnp.zeros(latents.shape, jnp.float32)
    inbox, pre_acts, branches = forward_phase(0, (inbox, pre_acts, zeros_acts), zeros_acts)
    skip_recv = mirror(branches)
    inputs_all, pre_acts, unused_branches = forward_phase(
        half_count, (inbox, pre_acts, branches), skip_recv
    )

    def backward_phase(top_section, carried, skip_fwd, skip_grad):

        def backward_tick_body(tick_index, loop_state):
            grad_inbox, normed_store, gpre_store, skip_grads_out = loop_state
            offset = top_section - section_index
            micro_index = tick_index - offset
            active = (
                (offset >= 0)
                & (offset < half_count)
                & (micro_index >= 0)
                & (micro_index < micro_count)
            )
            slot_index = jnp.clip(micro_index, 0, micro_count - 1)

            def backward_compute():
                inputs = inputs_all[slot_index].astype(jnp.float32) + skip_fwd[slot_index].astype(
                    jnp.float32
                )
                grad_out = grad_inbox[slot_index].astype(jnp.float32)
                grad_branch = grad_out + skip_grad[slot_index].astype(jnp.float32)
                return level_backward(inputs, weight, pre_acts[slot_index], grad_out, grad_branch)

            def backward_nothing():
                return (zero_field, zero_field, zero_field)

            outgoing, normed_b, grad_pre = lax.cond(active, backward_compute, backward_nothing)
            received = shifted(outgoing, "section", -1)
            recv_slot = tick_index - offset + 1
            receives = (
                (offset >= 1)
                & (offset <= half_count)
                & (recv_slot >= 0)
                & (recv_slot < micro_count)
            )
            grad_inbox = store_slot(
                grad_inbox, received, jnp.clip(recv_slot, 0, micro_count - 1), receives
            )
            normed_store = store_slot(normed_store, normed_b, slot_index, active)
            gpre_store = store_slot(gpre_store, grad_pre, slot_index, active)
            skip_grads_out = store_slot(skip_grads_out, outgoing, slot_index, active)
            return (grad_inbox, normed_store, gpre_store, skip_grads_out)

        return lax.fori_loop(0, tick_count, backward_tick_body, carried)

    grad_inbox = jnp.where(section_index == section_count - 1, cotangent, zeros_acts)
    grad_inbox, normed_store, gpre_store, skip_grads_out = backward_phase(
        section_count - 1, (grad_inbox, zeros_acts, zeros_acts, zeros_acts), skip_recv, zeros_acts
    )
    skip_grad_recv = mirror(skip_grads_out)
    grad_inbox, normed_store, gpre_store, unused_grads = backward_phase(
        half_count - 1,
        (grad_inbox, normed_store, gpre_store, zeros_acts),
        zeros_acts,
        skip_grad_recv,
    )
    summed = lax.psum_scatter(
        stored_weight_grad(normed_store, gpre_store).astype(jnp.bfloat16),
        "dp",
        scatter_dimension=3,
        tiled=True,
    ).astype(jnp.float32)
    row_total = (
        micro_count * latents.shape[1] * lax.axis_size("dp") * latents.shape[2] * latents.shape[3]
    )
    return (summed / math.sqrt(row_total))[None]


def solution(mesh):
    in_specs = (
        P(None, "dp", None, None, None),
        P(None, "dp", None, None, None),
        P("section", None, None, None, None),
        P(None, "dp"),
        P(),
    )
    out_specs = P("section", None, None, None, "dp")
    return jax.shard_map(
        on_device, mesh=mesh, in_specs=in_specs, out_specs=out_specs, check_vma=False
    )
```

profile of v0, /device:TPU:1, one launch (start us, length us, event | category | flops | bytes accessed | tf_op | source)
XLA Modules:
  0.0 1146.1 jit_solution(2567811564301204040)
XLA Ops:
  10.8 107.8 %while.76 = (s32[]{:T(128)}, bf16[2,1,8,8,640]{4,0,3,2,1:T(2,128)(2,1)S(1)}, f32[2,1,8,8,640]{4,0,3,2,1:T(2,128)S(1)}, bf16[2,1,8,8,640]{4,3,2,1,0:T(8,128)(2,1)...) while((s32[]{:T(128)}, ...), condition=%wide.region_4.5_spmd, body=%wide.region_0.4_spmd.sunk | while | flops 397230144 | bytes 11969947 | solution.py:162
  10.8 7.0 conditional.8
  24.0 7.0 conditional.8
  37.8 8.8 collective-permute-start
  58.7 8.6 collective-permute-start
  79.3 8.6 collective-permute-start
  102.4 11.3 collective-permute-start
  134.3 11.1 collective-permute-start.6
  154.1 88.3 %while.77 = (s32[]{:T(128)}, bf16[2,1,8,8,640]{4,0,3,2,1:T(2,128)(2,1)S(1)}, f32[2,1,8,8,640]{4,0,3,2,1:T(2,128)S(1)}, s32[]{:T(128)}, pred[]{:T(512)}, /*index=...) while((s32[]{:T(128)}, ...), condition=%wide.region_9.10_spmd, body=%wide.region_5.9_spmd.sunk | while | flops 397148224 | bytes 10167174 | solution.py:162
  187.8 6.4 collective-permute-start.1
  198.9 6.4 collective-permute-start.1
  232.2 7.1 collective-permute-start.1
  244.5 101.9 %while.78 = (s32[]{:T(128)}, bf16[2,1,8,8,640]{4,0,3,2,1:T(2,128)(2,1)S(1)}, bf16[2,1,8,8,640]{4,3,2,1,0:T(8,128)(2,1)}, bf16[2,1,8,8,640]{4,3,2,1,0:T(8,128)(2,...) while((s32[]{:T(128)}, ...), condition=%wide.region_15.16_spmd, body=%wide.region_10.15_spmd.sunk | while | flops 397721664 | bytes 12127959 | solution.py:214
  355.3 9.2 collective-permute-start.9
  369.0 93.4 %collective-permute-start.10 = (bf16[2,1,8,8,640]{4,0,3,2,1:T(2,128)(2,1)S(1)}, bf16[2,1,8,8,640]{4,0,3,2,1:T(2,128)(2,1)S(1)}, u32[]{:S(2)}, u32[]{:S(2)}) collective-permute-start(bf16[2,1,8,8,640]{4,0,3,2,1:T(2,128)(2,1)S(1)} %collective-permute-done.9), channel_id=1, source_target_pairs={{0,64},{64,0},{16,80},{80,16},{32,96},{96,32},{48,112},{112,48},{1... | collective-permute-start | bytes 491528 | tf_op jit(solution)/shard_map/ppermute | solution.py:18
  465.2 7.0 collective-permute-start.11
  475.0 158.2 %while.79 = (s32[]{:T(128)}, bf16[2,1,8,8,640]{4,0,3,2,1:T(2,128)(2,1)S(1)}, bf16[2,1,8,8,640]{4,3,2,1,0:T(8,128)(2,1)}, bf16[2,1,8,8,640]{4,3,2,1,0:T(8,128)(2,...) while((s32[]{:T(128)}, ...), condition=%wide.region_21.22_spmd, body=%wide.region_16.21_spmd.sunk | while | flops 397762624 | bytes 11062450 | solution.py:214
  531.4 62.1 %collective-permute-done.3 = bf16[1,8,8,640]{3,2,1,0:T(8,128)(2,1)} collective-permute-done((bf16[1,8,8,640]{3,2,1,0:T(8,128)(2,1)}, bf16[1,8,8,640]{3,2,1,0:T(8,128)(2,1)}, u32[]{:S(2)}, u32[]{:S(2)}) %collective-permute-start.3) | collective-permute-done | bytes 81952 | tf_op jit(solution)/shard_map/while/body/eval_jaxpr/ppermute | solution.py:24
  595.8 9.4 conditional.11
  598.0 6.6 multiply_reduce_fusion.1
  616.3 9.4 conditional.11
  618.5 6.6 multiply_reduce_fusion.1
  642.8 18.2 %copy.43 = bf16[3,3,640,640]{2,1,0,3:T(4,128)(2,1)} copy(bf16[3,3,640,640]{3,2,1,0:T(8,128)(2,1)} %pad_maximum_fusion) | data formatting | bytes 14745600 | tf_op jit(solution)/shard_map/stack | solution.py:67
  662.9 473.9 %all-reduce.4.cloned.1.call-done = bf16[3,3,640,640]{2,1,0,3:T(4,128)(2,1)} async-done(((bf16[3,3,640,640]{2,1,0,3:T(4,128)(2,1)}), bf16[3,3,640,640]{2,1,0,3:T(4,128)(2,1)}) %all-reduce.4.cloned.1.call-update) | async-done | bytes 7372816
  (592 shorter events, 397.6 us)
Async XLA Ops:
  6.5 1130.3 %all-reduce.4.cloned.1.call-start = ((), (), s32[]{:S(2)}) async-start(), calls=%async_computation | async-start | bytes 19660800
  37.8 12.3 %collective-permute-start = (bf16[1,8,8,640]{3,2,1,0:T(8,128)(2,1)S(1)}, bf16[1,8,8,640]{3,2,1,0:T(8,128)(2,1)S(1)}, u32[]{:S(2)}, u32[]{:S(2)}) collective-permute-start(bf16[1,8,8,640]{3,2,1,0:T(8,128)(2,1)S(1)} %copy.89), channel_id=1, source_target_pairs={{0,16},{16,32},{32,48},{48,64},{64,80},{80,96},{96,112},{112,128},... | collective-permute-start | bytes 245768 | tf_op jit(solution)/shard_map/while/body/eval_jaxpr/ppermute | solution.py:24
  58.7 12.1 %collective-permute-start = (bf16[1,8,8,640]{3,2,1,0:T(8,128)(2,1)S(1)}, bf16[1,8,8,640]{3,2,1,0:T(8,128)(2,1)S(1)}, u32[]{:S(2)}, u32[]{:S(2)}) collective-permute-start(bf16[1,8,8,640]{3,2,1,0:T(8,128)(2,1)S(1)} %copy.89), channel_id=1, source_target_pairs={{0,16},{16,32},{32,48},{48,64},{64,80},{80,96},{96,112},{112,128},... | collective-permute-start | bytes 245768 | tf_op jit(solution)/shard_map/while/body/eval_jaxpr/ppermute | solution.py:24
  79.3 12.1 %collective-permute-start = (bf16[1,8,8,640]{3,2,1,0:T(8,128)(2,1)S(1)}, bf16[1,8,8,640]{3,2,1,0:T(8,128)(2,1)S(1)}, u32[]{:S(2)}, u32[]{:S(2)}) collective-permute-start(bf16[1,8,8,640]{3,2,1,0:T(8,128)(2,1)S(1)} %copy.89), channel_id=1, source_target_pairs={{0,16},{16,32},{32,48},{48,64},{64,80},{80,96},{96,112},{112,128},... | collective-permute-start | bytes 245768 | tf_op jit(solution)/shard_map/while/body/eval_jaxpr/ppermute | solution.py:24
  102.4 14.8 %collective-permute-start = (bf16[1,8,8,640]{3,2,1,0:T(8,128)(2,1)S(1)}, bf16[1,8,8,640]{3,2,1,0:T(8,128)(2,1)S(1)}, u32[]{:S(2)}, u32[]{:S(2)}) collective-permute-start(bf16[1,8,8,640]{3,2,1,0:T(8,128)(2,1)S(1)} %copy.89), channel_id=1, source_target_pairs={{0,16},{16,32},{32,48},{48,64},{64,80},{80,96},{96,112},{112,128},... | collective-permute-start | bytes 245768 | tf_op jit(solution)/shard_map/while/body/eval_jaxpr/ppermute | solution.py:24
  134.3 14.1 %collective-permute-start.6 = (bf16[2,1,8,8,640]{4,0,3,2,1:T(2,128)(2,1)S(1)}, bf16[2,1,8,8,640]{4,0,3,2,1:T(2,128)(2,1)S(1)}, u32[]{:S(2)}, u32[]{:S(2)}) collective-permute-start(bf16[2,1,8,8,640]{4,0,3,2,1:T(2,128)(2,1)S(1)} %collective-permute-done.5), channel_id=1, source_target_pairs={{0,64},{64,0},{16,80},{80,16},{32,96},{96,32},{48,112},{112,48},{1... | collective-permute-start | bytes 491528 | tf_op jit(solution)/shard_map/ppermute | solution.py:18
  187.8 8.2 collective-permute-start.1
  198.9 8.2 collective-permute-start.1
  210.0 8.2 collective-permute-start.1
  221.1 8.2 collective-permute-start.1
  232.2 8.8 collective-permute-start.1
  245.2 9.7 collective-permute-start.2
  277.0 9.0 collective-permute-start.2
  288.1 10.4 collective-permute-start.2
  300.7 9.3 collective-permute-start.2
  312.1 8.4 collective-permute-start.2
  322.6 11.9 %collective-permute-start.2 = (bf16[1,8,8,640]{3,2,1,0:T(8,128)(2,1)}, bf16[1,8,8,640]{3,2,1,0:T(8,128)(2,1)}, u32[]{:S(2)}, u32[]{:S(2)}) collective-permute-start(bf16[1,8,8,640]{3,2,1,0:T(8,128)(2,1)} %get-tuple-element.1372), channel_id=1, source_target_pairs={{16,0},{32,16},{48,32},{64,48},{80,64},{96,80},{112,96},{128,112},... | collective-permute-start | bytes 245768 | tf_op jit(solution)/shard_map/while/body/eval_jaxpr/ppermute | solution.py:24
  336.6 8.4 collective-permute-start.2
  355.3 13.7 %collective-permute-start.9 = (bf16[2,1,8,8,640]{4,0,3,2,1:T(2,128)(2,1)S(1)}, bf16[2,1,8,8,640]{4,0,3,2,1:T(2,128)(2,1)S(1)}, u32[]{:S(2)}, u32[]{:S(2)}) collective-permute-start(bf16[2,1,8,8,640]{4,0,3,2,1:T(2,128)(2,1)S(1)} %collective-permute-done.8), channel_id=1, source_target_pairs={{0,32},{32,0},{16,48},{48,16},{64,96},{96,64},{80,112},{112,80},{1... | collective-permute-start | bytes 491528 | tf_op jit(solution)/shard_map/ppermute | solution.py:18
  369.0 96.1 %collective-permute-start.10 = (bf16[2,1,8,8,640]{4,0,3,2,1:T(2,128)(2,1)S(1)}, bf16[2,1,8,8,640]{4,0,3,2,1:T(2,128)(2,1)S(1)}, u32[]{:S(2)}, u32[]{:S(2)}) collective-permute-start(bf16[2,1,8,8,640]{4,0,3,2,1:T(2,128)(2,1)S(1)} %collective-permute-done.9), channel_id=1, source_target_pairs={{0,64},{64,0},{16,80},{80,16},{32,96},{96,32},{48,112},{112,48},{1... | collective-permute-start | bytes 491528 | tf_op jit(solution)/shard_map/ppermute | solution.py:18
  465.2 9.8 collective-permute-start.11
  516.2 9.0 collective-permute-start.3
  527.4 66.1 %collective-permute-start.3 = (bf16[1,8,8,640]{3,2,1,0:T(8,128)(2,1)}, bf16[1,8,8,640]{3,2,1,0:T(8,128)(2,1)}, u32[]{:S(2)}, u32[]{:S(2)}) collective-permute-start(bf16[1,8,8,640]{3,2,1,0:T(8,128)(2,1)} %copy.95), channel_id=1, source_target_pairs={{16,0},{32,16},{48,32},{64,48},{80,64},{96,80},{112,96},{128,112},... | collective-permute-start | bytes 245768 | tf_op jit(solution)/shard_map/while/body/eval_jaxpr/ppermute | solution.py:24
  605.8 8.2 collective-permute-start.3
  (34 other events, 172.4 us)
Sparse Core Ops, SparseCore 0:
  661.1 475.6 all-reduce.3
where the time goes:
time: 1150 us
  waiting for transfers between devices  596 us (52%)
  starting transfers between devices  253 us (22%)
  local copies, waits for them, and re-layouts  194 us (17%)
  other arithmetic  51.6 us (4%)
  matrix products  32.2 us (3%)
  between operations  14.3 us (1%)
    unnamed x2, waiting for transfers between devices  474 us
    ppermute x8, starting transfers between devices, from_partner(): return lax.ppermute(block, axis, route)  135 us
    ppermute x36, starting transfers between devices, shifted(): return lax.ppermute(x, axis, pairs)  118 us
    ppermute x36, waiting for transfers between devices, shifted(): return lax.ppermute(x, axis, pairs)  95.7 us
    dynamic_update_slice x54, local copies, waits for them, and re-layouts, store_slot(): lax.dynamic_update_index_in_dim(buffer, jnp.where(enabled, update, curren...  68.9 us
    dynamic_slice x99, local copies, waits for them, and re-layouts, store_slot(): current = lax.dynamic_index_in_dim(buffer, slot_index, 0, keepdims=False)  67.4 us
    dynamic_update_slice x36, other arithmetic, store_slot(): lax.dynamic_update_index_in_dim(buffer, jnp.where(enabled, update, curren...  32.8 us
    ppermute x8, waiting for transfers between devices, from_partner(): return lax.ppermute(block, axis, route)  26.3 us
  transfers between devices with their start and end apart: 45, of which 26 were waited for; matrix products, arithmetic and copies ran while one was open for 11% of the time, Pallas kernels for 0%

commit v1 on v0

v1 whole, which is shorter than its diff:
```python
import math

import jax
import jax.numpy as jnp
from jax import lax
from jax.experimental import pallas as pl
from jax.experimental.pallas import tpu as pltpu
from jax.sharding import PartitionSpec as P

EPS = 1e-05
SIDE = 8
PIX = SIDE * SIDE
ROWS = 48


def gather_taps(value, store):
    chans = value.shape[1]
    col = lax.broadcasted_iota(jnp.int32, (PIX, 1), 0) % SIDE
    edge = jnp.zeros((SIDE, chans), jnp.float32)
    left = jnp.where(col > 0, pltpu.roll(value, 1, 0), 0.0)
    right = jnp.where(col < SIDE - 1, pltpu.roll(value, PIX - 1, 0), 0.0)
    for kw, v in enumerate((left, value, right)):
        store(kw, jnp.concatenate([edge, v[: PIX - SIDE]], 0).astype(jnp.bfloat16))
        store(3 + kw, v.astype(jnp.bfloat16))
        store(6 + kw, jnp.concatenate([v[SIDE:], edge], 0).astype(jnp.bfloat16))


def column_blocks(chans):
    return [(a, min(a + 256, chans)) for a in range(0, chans, 256)]


def make_kernel(sections, replicas, chans, share, scale):
    half = sections // 2
    xs = replicas // 4

    def kernel(
        times_ref, lat_ref, cot_ref, w_hbm, table_hbm, out_ref,
        w, wt, table, lhs, inbox, skip, fout, sout, gin, dskip, gout,
        normed, inv, slope, gpre, gtrans, pack, shares, gathered, amat,
        load_sem, in_sem, f_send, f_recv, s_send, s_recv, g_send, g_recv, d_send, d_recv,
        a_send, a_recv, b_send, b_recv, c_send, c_recv, p_send, p_recv,
    ):
        s = lax.axis_index("section")
        d = lax.axis_index("dp")
        core = lax.rem(d, 2)
        zh = lax.rem(d // 2, 2)
        x = d // 4
        place = core * (replicas // 2) + x * 2 + zh

        def at(dst_s, dst_d):
            return {"section": dst_s, "dp": dst_d}

        def replica(px, pz, pc):
            return px * 4 + pz * 2 + pc

        nxt = jnp.minimum(s + 1, sections - 1)
        prv = jnp.maximum(s - 1, 0)
        mir = sections - 1 - s
        first, last = s == 0, s == sections - 1
        far = (s != half - 1) & (s != half)

        load_w = pltpu.make_async_copy(w_hbm, w, load_sem.at[0])
        load_t = pltpu.make_async_copy(table_hbm, table, load_sem.at[1])
        load_w.start()
        load_t.start()

        barrier = pltpu.get_barrier_semaphore()

        def greet(k, _):
            to = lax.rem(d + k, replicas)
            pl.semaphore_signal(barrier, inc=1, device_id=at(s, to))
            return None

        lax.fori_loop(1, replicas, greet, None)

        @pl.when(jnp.logical_not(first))
        def _():
            pl.semaphore_signal(barrier, inc=1, device_id=at(prv, d))

        @pl.when(jnp.logical_not(last))
        def _():
            pl.semaphore_signal(barrier, inc=1, device_id=at(nxt, d))

        @pl.when(far)
        def _():
            pl.semaphore_signal(barrier, inc=1, device_id=at(mir, d))

        @pl.when(first)
        def _():
            load = pltpu.make_async_copy(lat_ref, inbox, in_sem)
            load.start()
            load.wait()

        @pl.when(last)
        def _():
            load = pltpu.make_async_copy(cot_ref, gin, in_sem)
            load.start()
            load.wait()

        @pl.when(s <= half)
        def _():
            skip[...] = jnp.zeros_like(skip)

        @pl.when(s >= half - 1)
        def _():
            dskip[...] = jnp.zeros_like(dskip)

        load_w.wait()
        load_t.wait()
        pl.semaphore_wait(
            barrier,
            replicas - 1
            + jnp.where(first, 0, 1)
            + jnp.where(last, 0, 1)
            + jnp.where(far, 1, 0),
        )

        def turn_weights():
            def turn(t, _):
                src = pl.multiple_of(t * chans, chans)
                dst = pl.multiple_of((8 - t) * chans, chans)
                for r in range(0, chans, 128):
                    block = w[pl.ds(src + r, 128), :]
                    wt[pl.ds(dst, chans), r : r + 128] = block.T
                return None

            lax.fori_loop(0, 9, turn, None)

        early = s >= 4

        @pl.when(early)
        def _():
            turn_weights()

        def put(t, v):
            lhs[:, t * chans : (t + 1) * chans] = v

        def copy_f(m):
            return pltpu.make_async_remote_copy(
                src_ref=fout.at[m], dst_ref=inbox.at[m], send_sem=f_send.at[m], recv_sem=f_recv.at[m],
                device_id=at(nxt, d))

        def copy_s(m):
            return pltpu.make_async_remote_copy(
                src_ref=sout.at[m], dst_ref=skip.at[m], send_sem=s_send.at[m], recv_sem=s_recv.at[m],
                device_id=at(mir, d))

        def copy_g(m):
            return pltpu.make_async_remote_copy(
                src_ref=gout.at[m], dst_ref=gin.at[m], send_sem=g_send.at[m], recv_sem=g_recv.at[m],
                device_id=at(prv, d))

        def copy_d(m):
            return pltpu.make_async_remote_copy(
                src_ref=gout.at[m], dst_ref=dskip.at[m], send_sem=d_send.at[m], recv_sem=d_recv.at[m],
                device_id=at(mir, d))

        def forward(m, _):
            @pl.when(jnp.logical_not(first))
            def _():
                copy_f(m).wait_recv()

            @pl.when(s > half)
            def _():
                copy_s(m).wait_recv()

            value = inbox[m].astype(jnp.float32) + skip[m].astype(jnp.float32)
            inv_rms = lax.rsqrt(jnp.mean(value * value, axis=-1, keepdims=True) + EPS)
            norm = value * inv_rms
            gather_taps(norm, put)
            step = times_ref[m, 0]
            emb = table[pl.ds(step, 1), :]
            for a, b in column_blocks(chans):
                pre = jnp.dot(lhs[...], w[:, a:b], preferred_element_type=jnp.float32) + emb[:, a:b]
                sig = jax.nn.sigmoid(pre)
                branch = pre * sig
                result = value[:, a:b] + branch
                branch_b = branch.astype(jnp.bfloat16)
                result = result.astype(jnp.bfloat16).astype(jnp.float32)
                result = result + jnp.where(s == half - 1, branch_b.astype(jnp.float32), 0.0)
                fout[m, :, a:b] = result.astype(jnp.bfloat16)
                sout[m, :, a:b] = branch_b
                slope[m, :, a:b] = sig * (1.0 + pre * (1.0 - sig))

            @pl.when(jnp.logical_not(last))
            def _():
                copy_f(m).start()

            @pl.when(s < half - 1)
            def _():
                copy_s(m).start()

            normed[m] = norm
            inv[m] = jnp.broadcast_to(inv_rms, (PIX, 128))
            gathered[place, pl.ds(pl.multiple_of(m * PIX, PIX), PIX), :] = norm.astype(jnp.bfloat16)
            return None

        lax.fori_loop(0, 2, forward, None)

        @pl.when(jnp.logical_not(early))
        def _():
            turn_weights()

        def copy_a():
            mine = gathered.at[place]
            return pltpu.make_async_remote_copy(
                src_ref=mine, dst_ref=mine, send_sem=a_send, recv_sem=a_recv,
                device_id=at(s, replica(x, 1 - zh, core)))

        def copy_b(k):
            mine = gathered.at[pl.ds(core * (replicas // 2) + x * 2, 2)]
            return pltpu.make_async_remote_copy(
                src_ref=mine, dst_ref=mine, send_sem=b_send.at[k - 1], recv_sem=b_recv.at[k - 1],
                device_id=at(s, replica(lax.rem(x + k, xs), zh, core)))

        def wait_b(k):
            theirs = lax.rem(x + xs - k, xs)
            part = gathered.at[pl.ds(core * (replicas // 2) + theirs * 2, 2)]
            pltpu.make_async_remote_copy(
                src_ref=part, dst_ref=part, send_sem=b_send.at[k - 1], recv_sem=b_recv.at[k - 1],
                device_id=at(s, replica(theirs, zh, core))).wait_recv()

        def copy_c(c):
            part = gathered.at[pl.ds(c * (replicas // 2), replicas // 2)]
            return pltpu.make_async_remote_copy(
                src_ref=part, dst_ref=part, send_sem=c_send, recv_sem=c_recv,
                device_id=at(s, replica(x, zh, 1 - core)))

        def gather_all():
            theirs = gathered.at[core * (replicas // 2) + x * 2 + (1 - zh)]
            copy_a().start()
            pltpu.make_async_remote_copy(
                src_ref=theirs, dst_ref=theirs, send_sem=a_send, recv_sem=a_recv,
                device_id=at(s, replica(x, 1 - zh, core))).wait_recv()
            for k in range(1, xs):
                copy_b(k).start()
            for k in range(1, xs):
                wait_b(k)
            copy_c(core).start()
            copy_c(1 - core).wait_recv()
            copy_a().wait_send()
            for k in range(1, xs):
                copy_b(k).wait_send()
            copy_c(core).wait_send()

        soon = s < sections - 3

        @pl.when(soon)
        def _():
            gather_all()

        factor = jnp.where(s == half - 1, 2.0, 1.0).astype(jnp.float32)

        def backward(m, _):
            @pl.when(jnp.logical_not(last))
            def _():
                copy_g(m).wait_recv()

            @pl.when(s < half - 1)
            def _():
                copy_d(m).wait_recv()

            grad = gin[m].astype(jnp.float32)
            branch_grad = grad * factor + dskip[m].astype(jnp.float32)
            grad_pre = (branch_grad * slope[m]).astype(jnp.bfloat16).astype(jnp.float32)
            gather_taps(grad_pre, put)
            gpre[pl.ds(pl.multiple_of(m * PIX, PIX), PIX), :] = grad_pre
            parts = [
                jnp.dot(lhs[...], wt[:, a:b], preferred_element_type=jnp.float32)
                for a, b in column_blocks(chans)
            ]
            gn = jnp.concatenate(parts, axis=1)
            norm = normed[m]
            inner = jnp.mean(gn * norm, axis=-1, keepdims=True)
            gout[m] = (grad + inv[m][:, :1] * (gn - norm * inner)).astype(jnp.bfloat16)

            @pl.when(jnp.logical_not(first))
            def _():
                copy_g(m).start()

            @pl.when(s > half)
            def _():
                copy_d(m).start()

            return None

        lax.fori_loop(0, 2, backward, None)

        for r in range(0, chans, 128):
            gtrans[r : r + 128, :] = gpre[:, r : r + 128].T
        pad = jnp.zeros((ROWS - share, 2 * PIX), jnp.float32)
        for j in range(replicas):
            part = jnp.concatenate([gtrans[share * j : share * (j + 1), :], pad], 0)
            pack[j] = part.astype(jnp.bfloat16)

        def copy_p(to):
            return pltpu.make_async_remote_copy(
                src_ref=pack.at[to], dst_ref=shares.at[place], send_sem=p_send.at[to],
                recv_sem=p_recv.at[place], device_id=at(s, to))

        def send_share(k, _):
            copy_p(lax.rem(d + k, replicas)).start()
            return None

        lax.fori_loop(1, replicas, send_share, None)
        shares[place] = pack[d]

        @pl.when(jnp.logical_not(soon))
        def _():
            gather_all()

        def wait_share(k, _):
            slot = lax.rem(place + k, replicas)
            pltpu.make_async_remote_copy(
                src_ref=pack.at[0], dst_ref=shares.at[slot], send_sem=p_send.at[0],
                recv_sem=p_recv.at[slot], device_id=at(s, lax.rem(d + 1, replicas))).wait_recv()
            return None

        lax.fori_loop(1, replicas, wait_share, None)

        lane = lax.broadcasted_iota(jnp.int32, (1, 2 * PIX), 1)
        row, col = (lane // SIDE) % SIDE, lane % SIDE
        keep = []
        for kh in range(3):
            for kw in range(3):
                r, c = row - (kh - 1), col - (kw - 1)
                keep.append((r >= 0) & (r < SIDE) & (c >= 0) & (c < SIDE))
        for b in range(replicas):
            block = shares[b].astype(jnp.float32)
            for t in range(9):
                shift = (SIDE * (t // 3 - 1) + t % 3 - 1) % (2 * PIX)
                moved = pltpu.roll(block, shift, 1) if shift else block
                moved = jnp.where(keep[t], moved, 0.0)
                amat[ROWS * t : ROWS * (t + 1), 2 * PIX * b : 2 * PIX * (b + 1)] = moved.astype(jnp.bfloat16)
        rhs = gathered[...].reshape(replicas * 2 * PIX, chans)
        for a, b in column_blocks(chans):
            total = jnp.dot(amat[...], rhs[:, a:b], preferred_element_type=jnp.float32) * scale
            for t in range(9):
                out_ref[t, :, a:b] = total[ROWS * t : ROWS * t + share]

        def drain(m, _):
            @pl.when(jnp.logical_not(last))
            def _():
                copy_f(m).wait_send()

            @pl.when(s < half - 1)
            def _():
                copy_s(m).wait_send()

            @pl.when(jnp.logical_not(first))
            def _():
                copy_g(m).wait_send()

            @pl.when(s > half)
            def _():
                copy_d(m).wait_send()

            return None

        lax.fori_loop(0, 2, drain, None)

        def drain_share(k, _):
            copy_p(lax.rem(d + k, replicas)).wait_send()
            return None

        lax.fori_loop(1, replicas, drain_share, None)

    return kernel


def on_device(latents, cotangent, conv_weight, timesteps, time_table):
    sections = lax.axis_size("section")
    replicas = lax.axis_size("dp")
    micro, samples, side_h, side_w, chans = latents.shape
    share = chans // replicas
    scale = 1.0 / math.sqrt(micro * samples * replicas * side_h * side_w)
    fields = (micro, PIX, chans)
    dma = pltpu.SemaphoreType.DMA
    anyspace = pl.BlockSpec(memory_space=pl.ANY)
    bf, f32 = jnp.bfloat16, jnp.float32
    out = pl.pallas_call(
        make_kernel(sections, replicas, chans, share, scale),
        out_shape=jax.ShapeDtypeStruct((9, share, chans), f32),
        in_specs=[pl.BlockSpec(memory_space=pltpu.SMEM), anyspace, anyspace, anyspace, anyspace],
        out_specs=pl.BlockSpec(memory_space=pltpu.VMEM),
        scratch_shapes=[
            pltpu.VMEM((9 * chans, chans), bf),
            pltpu.VMEM((9 * chans, chans), bf),
            pltpu.VMEM(time_table.shape, f32),
            pltpu.VMEM((PIX, 9 * chans), bf),
            pltpu.VMEM(fields, bf),
            pltpu.VMEM(fields, bf),
            pltpu.VMEM(fields, bf),
            pltpu.VMEM(fields, bf),
            pltpu.VMEM(fields, bf),
            pltpu.VMEM(fields, bf),
            pltpu.VMEM(fields, bf),
            pltpu.VMEM(fields, f32),
            pltpu.VMEM((micro, PIX, 128), f32),
            pltpu.VMEM(fields, f32),
            pltpu.VMEM((micro * PIX, chans), f32),
            pltpu.VMEM((chans, micro * PIX), f32),
            pltpu.VMEM((replicas, ROWS, micro * PIX), bf),
            pltpu.VMEM((replicas, ROWS, micro * PIX), bf),
            pltpu.VMEM((replicas, micro * PIX, chans), bf),
            pltpu.VMEM((9 * ROWS, replicas * micro * PIX), bf),
            dma((2,)), dma, dma((2,)), dma((2,)), dma((2,)), dma((2,)), dma((2,)), dma((2,)), dma((2,)), dma((2,)),
            dma, dma, dma((replicas // 4 - 1,)), dma((replicas // 4 - 1,)), dma, dma,
            dma((replicas,)), dma((replicas,)),
        ],
        compiler_params=pltpu.CompilerParams(
            collective_id=0, has_side_effects=True, vmem_limit_bytes=56 * 2**20
        ),
        name="levels",
    )(
        timesteps,
        latents.reshape(fields),
        cotangent.reshape(fields),
        conv_weight.reshape(9 * chans, chans),
        time_table,
    )
    return jnp.swapaxes(out, 1, 2).reshape(1, 3, 3, chans, share)


def solution(mesh):
    in_specs = (
        P(None, "dp", None, None, None),
        P(None, "dp", None, None, None),
        P("section", None, None, None, None),
        P(None, "dp"),
        P(),
    )
    out_specs = P("section", None, None, None, "dp")
    return jax.shard_map(
        on_device, mesh=mesh, in_specs=in_specs, out_specs=out_specs, check_vma=False
    )
```

time: 1150 us -> 204 us (0.18)
  waiting for transfers between devices: 596 us -> 0 us
  starting transfers between devices: 253 us -> 0 us
  Pallas kernels: 0 us -> 201 us
  local copies, waits for them, and re-layouts: 194 us -> 3.46 us
  other arithmetic: 51.6 us -> 0 us
  matrix products: 32.2 us -> 0 us
  between operations: 14.3 us -> 0.01 us
    unnamed x2 -> x0, waiting for transfers between devices: 474 us -> none
    ppermute x44 -> x0, starting transfers between devices: 253 us -> none  [the longest x8 135 us: from_partner(): return lax.ppermute(block, axis, route)]
    pallas_call x0 -> x1, Pallas kernels: none -> 201 us  [on_device(): pl.pallas_call(make_kernel(sections, replicas, chans, share, scale), out_...]
    ppermute x44 -> x0, waiting for transfers between devices: 122 us -> none  [the longest x36 95.7 us: shifted(): return lax.ppermute(x, axis, pairs)]
    dynamic_update_slice x54 -> x0, local copies, waits for them, and re-layouts: 68.9 us -> none  [store_slot(): lax.dynamic_update_index_in_dim(buffer, jnp.where(enabled, update, curren...]
    dynamic_slice x101 -> x0, local copies, waits for them, and re-layouts: 67.4 us -> none  [the longest x99 67.4 us: store_slot(): current = lax.dynamic_index_in_dim(buffer, slot_index, 0, keepdims=False)]
    dynamic_update_slice x36 -> x0, other arithmetic: 32.8 us -> none  [store_slot(): lax.dynamic_update_index_in_dim(buffer, jnp.where(enabled, update, curren...]
    conv_general_dilated x4 -> x0, matrix products: 25.8 us -> none  [the longest x2 13.2 us: conv_input_grad(): lax.conv_general_dilated(grad_b, flipped, (1, 1), 'SAME', dimension_numbe...]
  transfers between devices with their start and end apart: 45 -> 0, of which waited for: 26 -> 0; matrix products, arithmetic and copies ran while one was open for 11% -> 0% of each run, Pallas kernels for 0% -> 0%
where the time goes in v1:
time: 204 us
  Pallas kernels  201 us (99%)
  local copies, waits for them, and re-layouts  3.46 us (2%)
    pallas_call x1, Pallas kernels, on_device(): pl.pallas_call(make_kernel(sections, replicas, chans, share, scale), out_...  201 us

profile of v1, /device:TPU:1, one launch (start us, length us, event | category | flops | bytes accessed | tf_op | source)
XLA Modules:
  0.0 204.3 jit_solution(2376734546130264908)
XLA Ops:
  0.0 1.3 copy.6.times_ref
  1.3 200.8 %levels.1 = f32[9,40,640]{2,1,0:T(8,128)} custom-call(s32[2,1]{1,0:T(2,128)} %copy.6.times_ref, bf16[2,64,640]{2,1,0:T(8,128)(2,1)} %bitcast.8, bf16[2,64,640]{2,1,0:T(8,128)(2,1)} %bitcast.9, bf16[5760,640]{1,0:T(8,128)(2,1)} %bitcast.6, f32[1000,640]{1,0:T(8,128)} %table_hbm.1), custom_call_target="tpu_custom_call" | custom-call | tf_op jit(solution)/shard_map/levels/pallas_call | solution.py:381
  202.1 2.2 %copy.8 = f32[1,3,3,640,40]{3,4,2,1,0:T(8,128)} copy(f32[1,3,3,640,40]{3,4,2,1,0:T(8,128)} %bitcast.7) | data formatting | bytes 1843200

commit v2 on v1

v2 whole, which is shorter than its diff:
```python
import math

import jax
import jax.numpy as jnp
from jax import lax
from jax.experimental import pallas as pl
from jax.experimental.pallas import tpu as pltpu
from jax.sharding import PartitionSpec as P

EPS = 1e-05
SIDE = 8
PIX = SIDE * SIDE
PAIR_FROM = 8
PACK_ROWS = 32
ROWS = 48


def gather_taps(value, store):
    chans = value.shape[1]
    col = lax.broadcasted_iota(jnp.int32, (PIX, 1), 0) % SIDE
    edge = jnp.zeros((SIDE, chans), jnp.float32)
    left = jnp.where(col > 0, pltpu.roll(value, 1, 0), 0.0)
    right = jnp.where(col < SIDE - 1, pltpu.roll(value, PIX - 1, 0), 0.0)
    for kw, v in enumerate((left, value, right)):
        store(kw, jnp.concatenate([edge, v[: PIX - SIDE]], 0).astype(jnp.bfloat16))
        store(3 + kw, v.astype(jnp.bfloat16))
        store(6 + kw, jnp.concatenate([v[SIDE:], edge], 0).astype(jnp.bfloat16))


def column_blocks(chans):
    return [(a, min(a + 256, chans)) for a in range(0, chans, 256)]


def make_kernel(sections, replicas, chans, share, scale, pair_from):
    half = sections // 2
    xs = replicas // 4
    lanes = 2 * PIX
    taps = 9 * chans

    def kernel(
        times_hbm, lat_ref, cot_ref, w_hbm, table_hbm, out_ref,
        times, w, wt, table, lhs, inbox, skip, fout, sout, gin, dskip, gout,
        state, gpre, gtrans, pack, shares, gathered, nstage, amat,
        load_sem, in_sem, f_send, f_recv, s_send, s_recv, g_send, g_recv, d_send, d_recv,
        a_send, a_recv, b_send, b_recv, c_send, c_recv, p_send, p_recv,
        n_send, n_recv, t_send, t_recv, z_send, z_recv, x_send, x_recv, y_send, y_recv, go,
    ):
        s = lax.axis_index("section")
        d = lax.axis_index("dp")
        core = lax.rem(d, 2)
        zh = lax.rem(d // 2, 2)
        x = d // 4
        place = core * (replicas // 2) + x * 2 + zh
        pair, e = s // 2, lax.rem(s, 2)
        mate = s + 1 - 2 * e
        line_len = 4
        line = lax.rem(s, line_len)
        top_line = s >= sections - line_len
        hop = s < pair_from

        def at(dst_s, dst_d):
            return {"section": dst_s, "dp": dst_d}

        def replica(px, pz, pc):
            return px * 4 + pz * 2 + pc

        def remote(src, dst, send, recv, dst_s, dst_d):
            return pltpu.make_async_remote_copy(
                src_ref=src, dst_ref=dst, send_sem=send, recv_sem=recv, device_id=at(dst_s, dst_d))

        load_w = pltpu.make_async_copy(w_hbm, w.at[e], load_sem.at[0])
        load_t = pltpu.make_async_copy(table_hbm, table, load_sem.at[1])
        load_i = pltpu.make_async_copy(times_hbm, times, load_sem.at[2])
        load_w.start()
        load_t.start()
        load_i.start()

        barrier = pltpu.get_barrier_semaphore()

        def greet(k, _):
            to = lax.rem(d + k, replicas)
            pl.semaphore_signal(barrier, inc=1, device_id=at(s, to))
            pl.semaphore_signal(barrier, inc=1, device_id=at(mate, to))
            return None

        pl.semaphore_signal(barrier, inc=1, device_id=at(mate, d))
        lax.fori_loop(1, replicas, greet, None)
        relations = [
            (pair < half - 1, jnp.minimum(s + 2, sections - 1)),
            (pair > 0, jnp.maximum(s - 2, 0)),
            ((e == 1) & (s < pair_from), jnp.minimum(s + 1, sections - 1)),
            ((e == 0) & (s > 0) & (s <= pair_from), jnp.maximum(s - 1, 0)),
            (s >= 0, 2 * (half - 1 - pair) + e),
            ((s < pair_from) | (s >= sections - pair_from), sections - 1 - s),
            (line == line_len - 1, jnp.maximum(s - line_len + 1, 0)),
            (line == 0, jnp.minimum(s + line_len - 1, sections - 1)),
        ]
        expected = 2 * replicas - 1
        for wanted, other in relations:
            expected = expected + jnp.where(wanted, 1, 0)

            @pl.when(wanted)
            def _():
                pl.semaphore_signal(barrier, inc=1, device_id=at(other, d))

        @pl.when(s == 0)
        def _():
            load = pltpu.make_async_copy(lat_ref, inbox, in_sem)
            load.start()
            load.wait()

        @pl.when(pair == half - 1)
        def _():
            load = pltpu.make_async_copy(cot_ref.at[e], gin.at[0], in_sem)
            load.start()
            load.wait()

        @pl.when(s < half + 2)
        def _():
            skip[0] = jnp.zeros_like(skip[0])

        @pl.when(s < half)
        def _():
            skip[1] = jnp.zeros_like(skip[1])

        @pl.when(s >= half)
        def _():
            dskip[0] = jnp.zeros_like(dskip[0])

        @pl.when(s >= half - 2)
        def _():
            dskip[1] = jnp.zeros_like(dskip[1])

        load_w.wait()
        load_t.wait()
        load_i.wait()
        pl.semaphore_wait(barrier, expected)

        def rows(start, count):
            return pl.ds(pl.multiple_of(start, 16), count)

        core_rows = taps // 2
        piece_v = core_rows // 8 // 16 * 16
        piece_u = core_rows // 4 - piece_v
        odd = lax.rem(x, 2)
        base_v = core * core_rows + 4 * piece_u
        sibling = replica(x, zh, 1 - core)

        def u_row(parity, k):
            return core * core_rows + (2 * parity + k) * piece_u

        def v_row(px):
            return base_v + px * piece_v

        def along(k):
            return replica(lax.rem(x + k, xs), zh, core)

        def z_piece(k):
            return v_row(x) if k == 0 else u_row(odd, k - 1)

        def copy_z(slot, k):
            ref = w.at[slot, rows(z_piece(k), piece_u if k else piece_v)]
            return remote(ref, ref, z_send.at[k], z_recv.at[k], mate, d)

        def copy_v(k, px):
            ref = w.at[1 - e, rows(v_row(px), piece_v)]
            return remote(ref, ref, x_send.at[k], x_recv.at[k], s, along(k))

        def copy_u(k, parity):
            ref = w.at[1 - e, rows(u_row(parity, k), piece_u)]
            return remote(ref, ref, x_send.at[xs + k], x_recv.at[xs + k], s, along(1 if k == 0 else xs - 1))

        def copy_y(k, c):
            ref = w.at[1 - e, rows(c * core_rows + k * 4 * piece_u, 4 * (piece_v if k else piece_u))]
            return remote(ref, ref, y_send.at[k], y_recv.at[k], s, sibling)

        def share_weights():
            for k in range(3):
                copy_z(e, k).start()

        def spread_weights():
            copy_z(1 - e, 0).wait_recv()
            for k in range(1, xs):
                copy_v(k, x).start()
            for k in range(2):
                copy_z(1 - e, 1 + k).wait_recv()
                copy_u(k, odd).start()
            for k in range(1, xs):
                copy_v(k, lax.rem(x + xs - k, xs)).wait_recv()
            copy_y(1, core).start()
            for k in range(2):
                copy_u(k, 1 - odd).wait_recv()
            copy_y(0, core).start()
            for k in range(2):
                copy_y(k, 1 - core).wait_recv()

        def turn_weights(slot):
            def turn(t, _):
                src = pl.multiple_of(t * chans, chans)
                dst = pl.multiple_of((8 - t) * chans, chans)
                for r in range(0, chans, 128):
                    block = w[slot, pl.ds(src + r, 128), :]
                    wt[slot, pl.ds(dst, chans), r : r + 128] = block.T
                return None

            lax.fori_loop(0, 9, turn, None)

        @pl.when(s >= pair_from)
        def _():
            share_weights()

        @pl.when(s >= line_len)
        def _():
            turn_weights(e)

        @pl.when(s >= pair_from)
        def _():
            spread_weights()

        @pl.when(top_line)
        def _():
            turn_weights(1 - e)

        def put(t, v):
            lhs[:, t * chans : (t + 1) * chans] = v

        def slot_and_micro(i):
            return jnp.where(hop, e, i), jnp.where(hop, i, e)

        def mirror(level, micro):
            return 2 * ((sections - 1 - level) // 2) + micro

        def sends_f(i):
            return hop | ((i == 1) & (pair < half - 1))

        def copy_f(i):
            to = jnp.where(hop, jnp.where(s == pair_from - 1, pair_from + i, s + 1), jnp.minimum(s + 2, sections - 1))
            slot = jnp.where(s < pair_from - 1, i, 0)
            return remote(fout.at[i], inbox.at[slot], f_send.at[i], f_recv.at[slot], to, d)

        def wait_f(i):
            remote(fout.at[i], inbox.at[i], f_send.at[i], f_recv.at[i], mate, d).wait_recv()

        def copy_s(i):
            slot, micro = slot_and_micro(i)
            return remote(
                sout.at[i], skip.at[1 - slot], s_send.at[i], s_recv.at[1 - slot], mirror(2 * pair + slot, micro), d)

        def wait_s(slot):
            remote(sout.at[0], skip.at[slot], s_send.at[0], s_recv.at[slot], mate, d).wait_recv()

        def sends_t(i):
            return hop & (i != e)

        def copy_t(slot):
            return remote(state.at[2], state.at[slot], t_send, t_recv, mate, d)

        def copy_n(micro):
            return remote(
                nstage, gathered.at[place, rows(micro * PIX, PIX)], n_send, n_recv, mate, d)

        def forward(i, _):
            slot, micro = slot_and_micro(i)
            level = 2 * pair + slot

            @pl.when(jnp.where(hop, jnp.where(s > 0, 1, 0), 1 - i) == 1)
            def _():
                wait_f(i)

            @pl.when(level > half)
            def _():
                wait_s(slot)

            value = inbox[i].astype(jnp.float32) + skip[slot].astype(jnp.float32)
            inv_rms = lax.rsqrt(jnp.mean(value * value, axis=-1, keepdims=True) + EPS)
            norm = value * inv_rms
            gather_taps(norm, put)
            step = times[micro, 0]
            emb = table[pl.ds(step, 1), :]
            saved = jnp.where(hop, jnp.where(i == e, e, 2), i)
            for a, b in column_blocks(chans):
                pre = jnp.dot(lhs[...], w[slot, :, a:b], preferred_element_type=jnp.float32) + emb[:, a:b]
                sig = jax.nn.sigmoid(pre)
                branch = pre * sig
                result = value[:, a:b] + branch
                branch_b = branch.astype(jnp.bfloat16)
                result = result.astype(jnp.bfloat16).astype(jnp.float32)
                result = result + jnp.where(level == half - 1, branch_b.astype(jnp.float32), 0.0)
                fout[i, :, a:b] = result.astype(jnp.bfloat16)
                sout[i, :, a:b] = branch_b
                state[saved, :, chans + a : chans + b] = sig * (1.0 + pre * (1.0 - sig))

            @pl.when(sends_f(i))
            def _():
                copy_f(i).start()

            @pl.when(level < half - 1)
            def _():
                copy_s(i).start()

            @pl.when(jnp.logical_not(hop) & (i == 0))
            def _():
                inbox[1] = fout[0]

            state[saved, :, :chans] = norm
            state[saved, :, 2 * chans :] = jnp.broadcast_to(inv_rms, (PIX, 128))
            norm_b = norm.astype(jnp.bfloat16)

            @pl.when(hop | (i == e))
            def _():
                gathered[place, rows(micro * PIX, PIX), :] = norm_b

            @pl.when(jnp.logical_not(hop) & (i != e))
            def _():
                nstage[...] = norm_b
                copy_n(e).start()

            @pl.when(sends_t(i))
            def _():
                copy_t(e).start()

            return None

        lax.fori_loop(0, 2, forward, None)

        @pl.when(jnp.logical_not(top_line) & (line == line_len - 1))
        def _():
            for k in range(1, line_len):
                pl.semaphore_signal(go, inc=1, device_id=at(s - k, d))

        @pl.when(s < line_len)
        def _():
            turn_weights(e)

        @pl.when(jnp.logical_not(top_line) & (line < line_len - 1))
        def _():
            pl.semaphore_wait(go, 1)

        @pl.when(hop)
        def _():
            share_weights()
            spread_weights()

        @pl.when(jnp.logical_not(top_line))
        def _():
            turn_weights(1 - e)

        group = replicas // 2

        def copy_a(pz):
            ref = gathered.at[core * group + x * 2 + pz]
            return remote(ref, ref, a_send, a_recv, s, replica(x, 1 - zh, core))

        def copy_b(k, px):
            ref = gathered.at[pl.ds(core * group + px * 2, 2)]
            return remote(
                ref, ref, b_send.at[k - 1], b_recv.at[k - 1], s, replica(lax.rem(x + k, xs), zh, core))

        def copy_c(c):
            ref = gathered.at[pl.ds(c * group, group)]
            return remote(ref, ref, c_send, c_recv, s, sibling)

        def gather_all():
            @pl.when(jnp.logical_not(hop))
            def _():
                copy_n(1 - e).wait_recv()

            copy_a(zh).start()
            copy_a(1 - zh).wait_recv()
            for k in range(1, xs):
                copy_b(k, x).start()
            for k in range(1, xs):
                copy_b(k, lax.rem(x + xs - k, xs)).wait_recv()
            copy_c(core).start()
            copy_c(1 - core).wait_recv()
            copy_a(zh).wait_send()
            for k in range(1, xs):
                copy_b(k, x).wait_send()
            copy_c(core).wait_send()

        soon = jnp.logical_not(top_line)

        @pl.when(soon)
        def _():
            gather_all()

        @pl.when(hop)
        def _():
            copy_t(1 - e).wait_recv()

        def copy_g():
            return remote(gout.at[1], gin.at[0], g_send, g_recv, jnp.maximum(s - 2, 0), d)

        def copy_d(i):
            return remote(
                gout.at[i], dskip.at[i], d_send.at[i], d_recv.at[i], mirror(2 * pair + 1 - i, e), d)

        def wait_d(slot):
            remote(gout.at[0], dskip.at[slot], d_send.at[0], d_recv.at[slot], mate, d).wait_recv()

        def backward(i, _):
            slot = 1 - i
            level = 2 * pair + slot

            @pl.when((i == 0) & (pair < half - 1))
            def _():
                copy_g().wait_recv()

            @pl.when(level < half - 1)
            def _():
                wait_d(slot)

            grad = gin[i].astype(jnp.float32)
            factor = jnp.where(level == half - 1, 2.0, 1.0).astype(jnp.float32)
            branch_grad = grad * factor + dskip[slot].astype(jnp.float32)
            grad_pre = (branch_grad * state[slot, :, chans : 2 * chans]).astype(jnp.bfloat16).astype(jnp.float32)
            gpre[slot] = grad_pre

            @pl.when(level > 0)
            def _():
                gather_taps(grad_pre, put)
                parts = [
                    jnp.dot(lhs[...], wt[slot, :, a:b], preferred_element_type=jnp.float32)
                    for a, b in column_blocks(chans)
                ]
                gn = jnp.concatenate(parts, axis=1)
                norm = state[slot, :, :chans]
                inner = jnp.mean(gn * norm, axis=-1, keepdims=True)
                inv_rms = state[slot, :, 2 * chans : 2 * chans + 1]
                gout[i] = (grad + inv_rms * (gn - norm * inner)).astype(jnp.bfloat16)

            @pl.when((i == 1) & (pair > 0))
            def _():
                copy_g().start()

            @pl.when(level > half)
            def _():
                copy_d(i).start()

            @pl.when(i == 0)
            def _():
                gin[1] = gout[0]

            return None

        lax.fori_loop(0, 2, backward, None)

        low = lax.broadcasted_iota(jnp.int32, (1, lanes), 1) < PIX
        top_rows = ROWS // 2
        pad = jnp.zeros((ROWS - share, lanes), jnp.float32)
        pad_rows = jnp.zeros((PACK_ROWS - top_rows, lanes), jnp.float32)

        def pack_level(slot):
            for r in range(0, chans, 128):
                block = gpre[slot, :, r : r + 128]
                gtrans[r : r + 128, :] = jnp.concatenate([block, block], 0).T
            for j in range(replicas):
                first = gtrans[share * j : share * j + top_rows, :]
                rest = jnp.concatenate([gtrans[share * j + top_rows : share * (j + 1), :], pad], 0)
                block = jnp.concatenate([jnp.where(low, first, rest), pad_rows], 0)
                pack[slot, j] = block.astype(jnp.bfloat16)

        def copy_p(slot, to):
            index = slot * replicas + to
            return remote(
                pack.at[slot, to], shares.at[e, place], p_send.at[index], p_recv.at[e * replicas + place],
                2 * pair + slot, to)

        def send_share(k, _):
            to = lax.rem(d + k, replicas)
            copy_p(e, to).start()
            copy_p(1 - e, to).start()
            return None

        def pack_loop(slot, _):
            pack_level(slot)
            return None

        lax.fori_loop(0, 2, pack_loop, None)
        copy_p(1 - e, d).start()
        lax.fori_loop(1, replicas, send_share, None)
        shares[e, place] = pack[e, d]

        @pl.when(jnp.logical_not(soon))
        def _():
            gather_all()

        def wait_share(micro, slot):
            remote(
                pack.at[0, 0], shares.at[micro, slot], p_send.at[0], p_recv.at[micro * replicas + slot], mate, d
            ).wait_recv()

        def wait_shares(k, _):
            slot = lax.rem(place + k, replicas)
            wait_share(0, slot)
            wait_share(1, slot)
            return None

        wait_share(1 - e, place)
        lax.fori_loop(1, replicas, wait_shares, None)

        lane = lax.broadcasted_iota(jnp.int32, (1, lanes), 1)
        row, col = (lane // SIDE) % SIDE, lane % SIDE
        keep = []
        for kh in range(3):
            for kw in range(3):
                r, c = row - (kh - 1), col - (kw - 1)
                keep.append((r >= 0) & (r < SIDE) & (c >= 0) & (c < SIDE))
        for b in range(replicas):
            one, two = (shares[m, b].astype(jnp.float32)[:top_rows] for m in range(2))
            block = jnp.concatenate(
                [jnp.where(low, one, pltpu.roll(two, PIX, 1)), jnp.where(low, pltpu.roll(one, PIX, 1), two)], 0)
            for t in range(9):
                shift = (SIDE * (t // 3 - 1) + t % 3 - 1) % lanes
                moved = pltpu.roll(block, shift, 1) if shift else block
                moved = jnp.where(keep[t], moved, 0.0)
                amat[ROWS * t : ROWS * (t + 1), lanes * b : lanes * (b + 1)] = moved.astype(jnp.bfloat16)
        rhs = gathered[...].reshape(replicas * lanes, chans)
        for a, b in column_blocks(chans):
            total = jnp.dot(amat[...], rhs[:, a:b], preferred_element_type=jnp.float32) * scale
            for t in range(9):
                out_ref[t, :, a:b] = total[ROWS * t : ROWS * t + share]

        for k in range(3):
            copy_z(e, k).wait_send()
        for k in range(1, xs):
            copy_v(k, x).wait_send()
        for k in range(2):
            copy_u(k, odd).wait_send()
            copy_y(k, core).wait_send()

        @pl.when(hop)
        def _():
            copy_t(e).wait_send()

        @pl.when(jnp.logical_not(hop))
        def _():
            copy_n(e).wait_send()

        @pl.when(pair > 0)
        def _():
            copy_g().wait_send()

        def drain(i, _):
            @pl.when(sends_f(i))
            def _():
                copy_f(i).wait_send()

            slot, micro = slot_and_micro(i)

            @pl.when(2 * pair + slot < half - 1)
            def _():
                copy_s(i).wait_send()

            @pl.when(2 * pair + 1 - i > half)
            def _():
                copy_d(i).wait_send()

            return None

        lax.fori_loop(0, 2, drain, None)

        def drain_share(k, _):
            to = lax.rem(d + k, replicas)
            copy_p(e, to).wait_send()
            copy_p(1 - e, to).wait_send()
            return None

        copy_p(1 - e, d).wait_send()
        lax.fori_loop(1, replicas, drain_share, None)

    return kernel


def on_device(latents, cotangent, conv_weight, timesteps, time_table):
    sections = lax.axis_size("section")
    replicas = lax.axis_size("dp")
    micro, samples, side_h, side_w, chans = latents.shape
    share = chans // replicas
    scale = 1.0 / math.sqrt(micro * samples * replicas * side_h * side_w)
    fields = (micro, PIX, chans)
    dma = pltpu.SemaphoreType.DMA
    anyspace = pl.BlockSpec(memory_space=pl.ANY)
    bf, f32 = jnp.bfloat16, jnp.float32
    out = pl.pallas_call(
        make_kernel(sections, replicas, chans, share, scale, PAIR_FROM),
        out_shape=jax.ShapeDtypeStruct((9, share, chans), f32),
        in_specs=[anyspace] * 5,
        out_specs=pl.BlockSpec(memory_space=pltpu.VMEM),
        scratch_shapes=[
            pltpu.SMEM(timesteps.shape, jnp.int32),
            pltpu.VMEM((2, 9 * chans, chans), bf),
            pltpu.VMEM((2, 9 * chans, chans), bf),
            pltpu.VMEM(time_table.shape, f32),
            pltpu.VMEM((PIX, 9 * chans), bf),
            pltpu.VMEM(fields, bf),
            pltpu.VMEM(fields, bf),
            pltpu.VMEM(fields, bf),
            pltpu.VMEM(fields, bf),
            pltpu.VMEM(fields, bf),
            pltpu.VMEM(fields, bf),
            pltpu.VMEM(fields, bf),
            pltpu.VMEM((3, PIX, 2 * chans + 128), f32),
            pltpu.VMEM((2, PIX, chans), f32),
            pltpu.VMEM((chans, micro * PIX), f32),
            pltpu.VMEM((2, replicas, PACK_ROWS, micro * PIX), bf),
            pltpu.VMEM((2, replicas, PACK_ROWS, micro * PIX), bf),
            pltpu.VMEM((replicas, micro * PIX, chans), bf),
            pltpu.VMEM((PIX, chans), bf),
            pltpu.VMEM((9 * ROWS, replicas * micro * PIX), bf),
            dma((3,)), dma, dma((2,)), dma((2,)), dma((2,)), dma((2,)), dma, dma, dma((2,)), dma((2,)),
            dma, dma, dma((replicas // 4 - 1,)), dma((replicas // 4 - 1,)), dma, dma,
            dma((2 * replicas,)), dma((2 * replicas,)),
            dma, dma, dma, dma, dma((3,)), dma((3,)), dma((6,)), dma((6,)), dma((2,)), dma((2,)),
            pltpu.SemaphoreType.REGULAR,
        ],
        compiler_params=pltpu.CompilerParams(
            collective_id=0, has_side_effects=True, vmem_limit_bytes=56 * 2**20
        ),
        name="levels",
    )(
        timesteps,
        latents.reshape(fields),
        cotangent.reshape(fields),
        conv_weight.reshape(9 * chans, chans),
        time_table,
    )
    return jnp.swapaxes(out, 1, 2).reshape(1, 3, 3, chans, share)


def solution(mesh):
    in_specs = (
        P(None, "dp", None, None, None),
        P(None, "dp", None, None, None),
        P("section", None, None, None, None),
        P(None, "dp"),
        P(),
    )
    out_specs = P("section", None, None, None, "dp")
    return jax.shard_map(
        on_device, mesh=mesh, in_specs=in_specs, out_specs=out_specs, check_vma=False
    )
```

time: 204 us -> 173 us (0.85)
  Pallas kernels: 201 us -> 169 us
    pallas_call x1, Pallas kernels: 201 us -> 169 us  [on_device(): pl.pallas_call(make_kernel(sections, replicas, chans, share, scale, PAIR_...]
where the time goes in v2:
time: 173 us
  Pallas kernels  169 us (98%)
  local copies, waits for them, and re-layouts  3.46 us (2%)
    pallas_call x1, Pallas kernels, on_device(): pl.pallas_call(make_kernel(sections, replicas, chans, share, scale, PAIR_...  169 us
    unnamed x2, local copies, waits for them, and re-layouts  3.46 us

profile of v2, /device:TPU:1, one launch (start us, length us, event | category | flops | bytes accessed | tf_op | source)
XLA Modules:
  0.0 172.8 jit_solution(2733758350164732721)
XLA Ops:
  0.0 1.3 copy.6.times_hbm
  1.3 169.3 %levels.1 = f32[9,40,640]{2,1,0:T(8,128)} custom-call(s32[2,1]{1,0:T(2,128)} %copy.6.times_hbm, bf16[2,64,640]{2,1,0:T(8,128)(2,1)} %bitcast.8, bf16[2,64,640]{2,1,0:T(8,128)(2,1)} %bitcast.9, bf16[5760,640]{1,0:T(8,128)(2,1)} %bitcast.6, f32[1000,640]{1,0:T(8,128)} %table_hbm.1), custom_call_target="tpu_custom_call" | custom-call | tf_op jit(solution)/shard_map/levels/pallas_call | solution.py:585
  170.6 2.2 %copy.8 = f32[1,3,3,640,40]{3,4,2,1,0:T(8,128)} copy(f32[1,3,3,640,40]{3,4,2,1,0:T(8,128)} %bitcast.7) | data formatting | bytes 1843200

commit v3 on v2

--- a/solution.py
+++ b/solution.py
@@ -43,7 +43,7 @@
         state, gpre, gtrans, pack, shares, gathered, nstage, amat,
         load_sem, in_sem, f_send, f_recv, s_send, s_recv, g_send, g_recv, d_send, d_recv,
         a_send, a_recv, b_send, b_recv, c_send, c_recv, p_send, p_recv,
-        n_send, n_recv, t_send, t_recv, z_send, z_recv, x_send, x_recv, y_send, y_recv, go,
+        n_send, n_recv, t_send, t_recv, z_send, z_recv, v_send, v_recv, u_send, u_recv, y_send, y_recv, go,
     ):
         s = lax.axis_index("section")
         d = lax.axis_index("dp")
@@ -131,66 +131,76 @@
         def _():
             dskip[1] = jnp.zeros_like(dskip[1])
 
-        load_w.wait()
-        load_t.wait()
-        load_i.wait()
         pl.semaphore_wait(barrier, expected)
 
         def rows(start, count):
             return pl.ds(pl.multiple_of(start, 16), count)
 
         core_rows = taps // 2
-        piece_v = core_rows // 8 // 16 * 16
-        piece_u = core_rows // 4 - piece_v
+        piece_v = core_rows // 16 // 16 * 16
+        all_v = 8 * piece_v
+        all_u = core_rows - all_v
+        cut_u = [all_u // 2 * k // 4 // 16 * 16 for k in range(5)]
+        size_u = [b - a for a, b in zip(cut_u, cut_u[1:])]
+        base_v = core * core_rows + all_u
         odd = lax.rem(x, 2)
-        base_v = core * core_rows + 4 * piece_u
         sibling = replica(x, zh, 1 - core)
 
         def u_row(parity, k):
-            return core * core_rows + (2 * parity + k) * piece_u
-
-        def v_row(px):
-            return base_v + px * piece_v
+            return core * core_rows + parity * (all_u // 2) + cut_u[k]
+
+        def v_row(px, k):
+            return base_v + (2 * px + k) * piece_v
 
         def along(k):
             return replica(lax.rem(x + k, xs), zh, core)
 
-        def z_piece(k):
-            return v_row(x) if k == 0 else u_row(odd, k - 1)
-
-        def copy_z(slot, k):
-            ref = w.at[slot, rows(z_piece(k), piece_u if k else piece_v)]
-            return remote(ref, ref, z_send.at[k], z_recv.at[k], mate, d)
-
-        def copy_v(k, px):
-            ref = w.at[1 - e, rows(v_row(px), piece_v)]
-            return remote(ref, ref, x_send.at[k], x_recv.at[k], s, along(k))
+        def copy_z(k):
+            row, count = (v_row(x, k), piece_v) if k < 2 else (u_row(odd, k - 2), size_u[k - 2])
+            return remote(
+                w_hbm.at[rows(row, count)], w.at[e, rows(row, count)], z_send.at[k], z_recv.at[k], mate, d)
+
+        def wait_z(k):
+            row, count = (v_row(x, k), piece_v) if k < 2 else (u_row(odd, k - 2), size_u[k - 2])
+            ref = w.at[1 - e, rows(row, count)]
+            remote(ref, ref, z_send.at[k], z_recv.at[k], mate, d).wait_recv()
+
+        def copy_v(n, k, px):
+            ref = w.at[1 - e, rows(v_row(px, k), piece_v)]
+            return remote(ref, ref, v_send.at[3 * k + n - 1], v_recv.at[3 * k + n - 1], s, along(n))
 
         def copy_u(k, parity):
-            ref = w.at[1 - e, rows(u_row(parity, k), piece_u)]
-            return remote(ref, ref, x_send.at[xs + k], x_recv.at[xs + k], s, along(1 if k == 0 else xs - 1))
+            ref = w.at[1 - e, rows(u_row(parity, k), size_u[k])]
+            return remote(ref, ref, u_send.at[k], u_recv.at[k], s, along(xs - 1 if k % 2 else 1))
 
         def copy_y(k, c):
-            ref = w.at[1 - e, rows(c * core_rows + k * 4 * piece_u, 4 * (piece_v if k else piece_u))]
+            row, count = (c * core_rows + all_u, all_v) if k == 0 else (c * core_rows, all_u)
+            ref = w.at[1 - e, rows(row, count)]
             return remote(ref, ref, y_send.at[k], y_recv.at[k], s, sibling)
 
         def share_weights():
-            for k in range(3):
-                copy_z(e, k).start()
-
-        def spread_weights():
-            copy_z(1 - e, 0).wait_recv()
-            for k in range(1, xs):
-                copy_v(k, x).start()
+            for k in range(6):
+                copy_z(k).start()
+
+        def spread_z():
             for k in range(2):
-                copy_z(1 - e, 1 + k).wait_recv()
+                wait_z(k)
+                for n in (1, xs - 1, 2):
+                    copy_v(n, k, x).start()
+
+        def spread_x():
+            for k in range(4):
+                wait_z(2 + k)
                 copy_u(k, odd).start()
-            for k in range(1, xs):
-                copy_v(k, lax.rem(x + xs - k, xs)).wait_recv()
+            for k in range(2):
+                for n in range(1, xs):
+                    copy_v(n, k, lax.rem(x + xs - n, xs)).wait_recv()
+            copy_y(0, core).start()
+            for k in range(4):
+                copy_u(k, 1 - odd).wait_recv()
             copy_y(1, core).start()
-            for k in range(2):
-                copy_u(k, 1 - odd).wait_recv()
-            copy_y(0, core).start()
+
+        def spread_y():
             for k in range(2):
                 copy_y(k, 1 - core).wait_recv()
 
@@ -209,13 +219,19 @@
         def _():
             share_weights()
 
+        load_w.wait()
+        load_t.wait()
+        load_i.wait()
+
         @pl.when(s >= line_len)
         def _():
             turn_weights(e)
 
         @pl.when(s >= pair_from)
         def _():
-            spread_weights()
+            spread_z()
+            spread_x()
+            spread_y()
 
         @pl.when(top_line)
         def _():
@@ -336,15 +352,6 @@
         def _():
             pl.semaphore_wait(go, 1)
 
-        @pl.when(hop)
-        def _():
-            share_weights()
-            spread_weights()
-
-        @pl.when(jnp.logical_not(top_line))
-        def _():
-            turn_weights(1 - e)
-
         group = replicas // 2
 
         def copy_a(pz):
@@ -360,33 +367,79 @@
             ref = gathered.at[pl.ds(c * group, group)]
             return remote(ref, ref, c_send, c_recv, s, sibling)
 
-        def gather_all():
-            @pl.when(jnp.logical_not(hop))
-            def _():
-                copy_n(1 - e).wait_recv()
-
+        def gather_a():
             copy_a(zh).start()
+
+        def gather_b():
             copy_a(1 - zh).wait_recv()
             for k in range(1, xs):
                 copy_b(k, x).start()
+
+        def gather_c():
             for k in range(1, xs):
                 copy_b(k, lax.rem(x + xs - k, xs)).wait_recv()
             copy_c(core).start()
             copy_c(1 - core).wait_recv()
-            copy_a(zh).wait_send()
-            for k in range(1, xs):
-                copy_b(k, x).wait_send()
-            copy_c(core).wait_send()
+
+        def gather_all():
+            copy_n(1 - e).wait_recv()
+            gather_a()
+            gather_b()
+            gather_c()
+
+        @pl.when(hop)
+        def _():
+            share_weights()
+            gather_a()
+            spread_z()
+            gather_b()
+            spread_x()
+            gather_c()
+            spread_y()
+
+        @pl.when(jnp.logical_not(top_line))
+        def _():
+            turn_weights(1 - e)
 
         soon = jnp.logical_not(top_line)
 
-        @pl.when(soon)
+        @pl.when(soon & jnp.logical_not(hop))
         def _():
             gather_all()
 
         @pl.when(hop)
         def _():
             copy_t(1 - e).wait_recv()
+
+        low = lax.broadcasted_iota(jnp.int32, (1, lanes), 1) < PIX
+        top_rows = ROWS // 2
+        pad = jnp.zeros((ROWS - share, lanes), jnp.float32)
+        pad_rows = jnp.zeros((PACK_ROWS - top_rows, lanes), jnp.float32)
+
+        def pack_level(slot):
+            for r in range(0, chans, 128):
+                block = gpre[slot, :, r : r + 128]
+                gtrans[r : r + 128, :] = jnp.concatenate([block, block], 0).T
+            for j in range(replicas):
+                first = gtrans[share * j : share * j + top_rows, :]
+                rest = jnp.concatenate([gtrans[share * j + top_rows : share * (j + 1), :], pad], 0)
+                block = jnp.concatenate([jnp.where(low, first, rest), pad_rows], 0)
+                pack[slot, j] = block.astype(jnp.bfloat16)
+
+        def copy_p(slot, to):
+            index = slot * replicas + to
+            return remote(
+                pack.at[slot, to], shares.at[e, place], p_send.at[index], p_recv.at[e * replicas + place],
+                2 * pair + slot, to)
+
+        def send_level(slot):
+            pack_level(slot)
+
+            def send_share(k, _):
+                copy_p(slot, lax.rem(d + k, replicas)).start()
+                return None
+
+            lax.fori_loop(jnp.where(slot == e, 1, 0), replicas, send_share, None)
 
         def copy_g():
             return remote(gout.at[1], gin.at[0], g_send, g_recv, jnp.maximum(s - 2, 0), d)
@@ -415,6 +468,10 @@
             branch_grad = grad * factor + dskip[slot].astype(jnp.float32)
             grad_pre = (branch_grad * state[slot, :, chans : 2 * chans]).astype(jnp.bfloat16).astype(jnp.float32)
             gpre[slot] = grad_pre
+
+            @pl.when(level == 1)
+            def _():
+                send_level(1)
 
             @pl.when(level > 0)
             def _():
@@ -445,40 +502,11 @@
 
         lax.fori_loop(0, 2, backward, None)
 
-        low = lax.broadcasted_iota(jnp.int32, (1, lanes), 1) < PIX
-        top_rows = ROWS // 2
-        pad = jnp.zeros((ROWS - share, lanes), jnp.float32)
-        pad_rows = jnp.zeros((PACK_ROWS - top_rows, lanes), jnp.float32)
-
-        def pack_level(slot):
-            for r in range(0, chans, 128):
-                block = gpre[slot, :, r : r + 128]
-                gtrans[r : r + 128, :] = jnp.concatenate([block, block], 0).T
-            for j in range(replicas):
-                first = gtrans[share * j : share * j + top_rows, :]
-                rest = jnp.concatenate([gtrans[share * j + top_rows : share * (j + 1), :], pad], 0)
-                block = jnp.concatenate([jnp.where(low, first, rest), pad_rows], 0)
-                pack[slot, j] = block.astype(jnp.bfloat16)
-
-        def copy_p(slot, to):
-            index = slot * replicas + to
-            return remote(
-                pack.at[slot, to], shares.at[e, place], p_send.at[index], p_recv.at[e * replicas + place],
-                2 * pair + slot, to)
-
-        def send_share(k, _):
-            to = lax.rem(d + k, replicas)
-            copy_p(e, to).start()
-            copy_p(1 - e, to).start()
-            return None
-
-        def pack_loop(slot, _):
-            pack_level(slot)
-            return None
-
-        lax.fori_loop(0, 2, pack_loop, None)
-        copy_p(1 - e, d).start()
-        lax.fori_loop(1, replicas, send_share, None)
+        @pl.when(pair > 0)
+        def _():
+            send_level(1)
+
+        send_level(0)
         shares[e, place] = pack[e, d]
 
         @pl.when(jnp.logical_not(soon))
@@ -521,13 +549,18 @@
             for t in range(9):
                 out_ref[t, :, a:b] = total[ROWS * t : ROWS * t + share]
 
-        for k in range(3):
-            copy_z(e, k).wait_send()
+        copy_a(zh).wait_send()
         for k in range(1, xs):
-            copy_v(k, x).wait_send()
+            copy_b(k, x).wait_send()
+        copy_c(core).wait_send()
+        for k in range(6):
+            copy_z(k).wait_send()
         for k in range(2):
+            for n in range(1, xs):
+                copy_v(n, k, x).wait_send()
+            copy_y(k, core).wait_send()
+        for k in range(4):
             copy_u(k, odd).wait_send()
-            copy_y(k, core).wait_send()
 
         @pl.when(hop)
         def _():
@@ -611,7 +644,7 @@
             dma((3,)), dma, dma((2,)), dma((2,)), dma((2,)), dma((2,)), dma, dma, dma((2,)), dma((2,)),
             dma, dma, dma((replicas // 4 - 1,)), dma((replicas // 4 - 1,)), dma, dma,
             dma((2 * replicas,)), dma((2 * replicas,)),
-            dma, dma, dma, dma, dma((3,)), dma((3,)), dma((6,)), dma((6,)), dma((2,)), dma((2,)),
+            dma, dma, dma, dma, dma((6,)), dma((6,)), dma((6,)), dma((6,)), dma((4,)), dma((4,)), dma((2,)), dma((2,)),
             pltpu.SemaphoreType.REGULAR,
         ],
         compiler_params=pltpu.CompilerParams(

time: 173 us -> 166 us (0.960)
  Pallas kernels: 169 us -> 162 us
    pallas_call x1, Pallas kernels: 169 us -> 162 us  [on_device(): pl.pallas_call(make_kernel(sections, replicas, chans, share, scale, PAIR_...]
where the time goes in v3:
time: 166 us
  Pallas kernels  162 us (98%)
  local copies, waits for them, and re-layouts  3.46 us (2%)
    pallas_call x1, Pallas kernels, on_device(): pl.pallas_call(make_kernel(sections, replicas, chans, share, scale, PAIR_...  162 us
    unnamed x2, local copies, waits for them, and re-layouts  3.46 us

profile of v3, /device:TPU:1, one launch (start us, length us, event | category | flops | bytes accessed | tf_op | source)
XLA Modules:
  0.0 165.7 jit_solution(8062710114937682816)
XLA Ops:
  0.0 1.3 copy.6.times_hbm
  1.3 162.2 %levels.1 = f32[9,40,640]{2,1,0:T(8,128)} custom-call(s32[2,1]{1,0:T(2,128)} %copy.6.times_hbm, bf16[2,64,640]{2,1,0:T(8,128)(2,1)} %bitcast.8, bf16[2,64,640]{2,1,0:T(8,128)(2,1)} %bitcast.9, bf16[5760,640]{1,0:T(8,128)(2,1)} %bitcast.6, f32[1000,640]{1,0:T(8,128)} %table_hbm.1), custom_call_target="tpu_custom_call" | custom-call | tf_op jit(solution)/shard_map/levels/pallas_call | solution.py:618
  163.6 2.2 %copy.8 = f32[1,3,3,640,40]{3,4,2,1,0:T(8,128)} copy(f32[1,3,3,640,40]{3,4,2,1,0:T(8,128)} %bitcast.7) | data formatting | bytes 1843200

commit v4 on v3

--- a/solution.py
+++ b/solution.py
@@ -291,7 +291,7 @@
             inv_rms = lax.rsqrt(jnp.mean(value * value, axis=-1, keepdims=True) + EPS)
             norm = value * inv_rms
             gather_taps(norm, put)
-            step = times[micro, 0]
+            step = times[0, micro]
             emb = table[pl.ds(step, 1), :]
             saved = jnp.where(hop, jnp.where(i == e, e, 2), i)
             for a, b in column_blocks(chans):
@@ -367,6 +367,8 @@
             ref = gathered.at[pl.ds(c * group, group)]
             return remote(ref, ref, c_send, c_recv, s, sibling)
 
+        tight = (s >= line_len) & jnp.logical_not(top_line)
+
         def gather_a():
             copy_a(zh).start()
 
@@ -392,20 +394,27 @@
             share_weights()
             gather_a()
             spread_z()
-            gather_b()
+
+            @pl.when(jnp.logical_not(tight))
+            def _():
+                gather_b()
+
             spread_x()
-            gather_c()
+
+            @pl.when(jnp.logical_not(tight))
+            def _():
+                gather_c()
+
             spread_y()
 
         @pl.when(jnp.logical_not(top_line))
         def _():
             turn_weights(1 - e)
 
-        soon = jnp.logical_not(top_line)
-
-        @pl.when(soon & jnp.logical_not(hop))
-        def _():
-            gather_all()
+        @pl.when(tight & jnp.logical_not(hop))
+        def _():
+            copy_n(1 - e).wait_recv()
+            gather_a()
 
         @pl.when(hop)
         def _():
@@ -432,14 +441,18 @@
                 pack.at[slot, to], shares.at[e, place], p_send.at[index], p_recv.at[e * replicas + place],
                 2 * pair + slot, to)
 
+        def share_dest(k):
+            return replica(
+                lax.rem(x + 1 + k // 2, xs), lax.rem(zh + 1 + k // (replicas // 2), 2), lax.rem(core + 1 + k, 2))
+
         def send_level(slot):
             pack_level(slot)
 
             def send_share(k, _):
-                copy_p(slot, lax.rem(d + k, replicas)).start()
+                copy_p(slot, share_dest(k)).start()
                 return None
 
-            lax.fori_loop(jnp.where(slot == e, 1, 0), replicas, send_share, None)
+            lax.fori_loop(0, jnp.where(slot == e, replicas - 1, replicas), send_share, None)
 
         def copy_g():
             return remote(gout.at[1], gin.at[0], g_send, g_recv, jnp.maximum(s - 2, 0), d)
@@ -509,9 +522,75 @@
         send_level(0)
         shares[e, place] = pack[e, d]
 
-        @pl.when(jnp.logical_not(soon))
+        @pl.when(tight)
+        def _():
+            gather_b()
+            gather_c()
+
+        @pl.when(top_line & (line < 2))
+        def _():
+            pl.semaphore_signal(go, inc=1, device_id=at(s + 2, d))
+
+        @pl.when(top_line & (line >= 2))
+        def _():
+            pl.semaphore_wait(go, 1)
+
+        @pl.when(top_line)
         def _():
             gather_all()
+
+        copy_a(zh).wait_send()
+        for k in range(1, xs):
+            copy_b(k, x).wait_send()
+        copy_c(core).wait_send()
+        for k in range(6):
+            copy_z(k).wait_send()
+        for k in range(2):
+            for n in range(1, xs):
+                copy_v(n, k, x).wait_send()
+            copy_y(k, core).wait_send()
+        for k in range(4):
+            copy_u(k, odd).wait_send()
+
+        @pl.when(hop)
+        def _():
+            copy_t(e).wait_send()
+
+        @pl.when(jnp.logical_not(hop))
+        def _():
+            copy_n(e).wait_send()
+
+        @pl.when(pair > 0)
+        def _():
+            copy_g().wait_send()
+
+        def drain(i, _):
+            @pl.when(sends_f(i))
+            def _():
+                copy_f(i).wait_send()
+
+            slot, micro = slot_and_micro(i)
+
+            @pl.when(2 * pair + slot < half - 1)
+            def _():
+                copy_s(i).wait_send()
+
+            @pl.when(2 * pair + 1 - i > half)
+            def _():
+                copy_d(i).wait_send()
+
+            return None
+
+        lax.fori_loop(0, 2, drain, None)
+
+        def drain_share(k, _):
+            to = lax.rem(d + k, replicas)
+            copy_p(e, to).wait_send()
+            copy_p(1 - e, to).wait_send()
+            return None
+
+        copy_p(1 - e, d).wait_send()
+        lax.fori_loop(1, replicas, drain_share, None)
 
         def wait_share(micro, slot):
             remote(
@@ -549,58 +628,6 @@
             for t in range(9):
                 out_ref[t, :, a:b] = total[ROWS * t : ROWS * t + share]
 
-        copy_a(zh).wait_send()
-        for k in range(1, xs):
-            copy_b(k, x).wait_send()
-        copy_c(core).wait_send()
-        for k in range(6):
-            copy_z(k).wait_send()
-        for k in range(2):
-            for n in range(1, xs):
-                copy_v(n, k, x).wait_send()
-            copy_y(k, core).wait_send()
-        for k in range(4):
-            copy_u(k, odd).wait_send()
-
-        @pl.when(hop)
-        def _():
-            copy_t(e).wait_send()
-
-        @pl.when(jnp.logical_not(hop))
-        def _():
-            copy_n(e).wait_send()
-
-        @pl.when(pair > 0)
-        def _():
-            copy_g().wait_send()
-
-        def drain(i, _):
-            @pl.when(sends_f(i))
-            def _():
-                copy_f(i).wait_send()
-
-            slot, micro = slot_and_micro(i)
-
-            @pl.when(2 * pair + slot < half - 1)
-            def _():
-                copy_s(i).wait_send()
-
-            @pl.when(2 * pair + 1 - i > half)
-            def _():
-                copy_d(i).wait_send()
-
-            return None
-
-        lax.fori_loop(0, 2, drain, None)
-
-        def drain_share(k, _):
-            to = lax.rem(d + k, replicas)
-            copy_p(e, to).wait_send()
-            copy_p(1 - e, to).wait_send()
-            return None
-
-        copy_p(1 - e, d).wait_send()
-        lax.fori_loop(1, replicas, drain_share, None)
 
     return kernel
 
@@ -621,7 +648,7 @@
         in_specs=[anyspace] * 5,
         out_specs=pl.BlockSpec(memory_space=pltpu.VMEM),
         scratch_shapes=[
-            pltpu.SMEM(timesteps.shape, jnp.int32),
+            pltpu.SMEM((1, micro), jnp.int32),
             pltpu.VMEM((2, 9 * chans, chans), bf),
             pltpu.VMEM((2, 9 * chans, chans), bf),
             pltpu.VMEM(time_table.shape, f32),
@@ -652,7 +679,7 @@
         ),
         name="levels",
     )(
-        timesteps,
+        timesteps.reshape(1, micro),
         latents.reshape(fields),
         cotangent.reshape(fields),
         conv_weight.reshape(9 * chans, chans),

time: 166 us -> 163 us (0.982)
    unnamed x2 -> x1, local copies, waits for them, and re-layouts: 3.46 us -> 2.16 us
where the time goes in v4:
time: 163 us
  Pallas kernels  161 us (99%)
  local copies, waits for them, and re-layouts  2.16 us (1%)
    pallas_call x1, Pallas kernels, on_device(): pl.pallas_call(make_kernel(sections, replicas, chans, share, scale, PAIR_...  161 us

profile of v4, /device:TPU:1, one launch (start us, length us, event | category | flops | bytes accessed | tf_op | source)
XLA Modules:
  0.0 163.3 jit_solution(7010771584789231871)
XLA Ops:
  0.0 161.2 %levels.1 = f32[9,40,640]{2,1,0:T(8,128)} custom-call(s32[1,2]{1,0:T(1,128)} %bitcast.11, bf16[2,64,640]{2,1,0:T(8,128)(2,1)} %bitcast.9, bf16[2,64,640]{2,1,0:T(8,128)(2,1)} %bitcast.10, bf16[5760,640]{1,0:T(8,128)(2,1)} %bitcast.7, f32[1000,640]{1,0:T(8,128)} %table_hbm.1), custom_call_target="tpu_custom_call" | custom-call | tf_op jit(solution)/shard_map/levels/pallas_call | solution.py:645
  161.2 2.2 %copy.7 = f32[1,3,3,640,40]{3,4,2,1,0:T(8,128)} copy(f32[1,3,3,640,40]{3,4,2,1,0:T(8,128)} %bitcast.8) | data formatting | bytes 1843200

commit v5 on v4

--- a/solution.py
+++ b/solution.py
@@ -310,10 +310,6 @@
             def _():
                 copy_f(i).start()
 
-            @pl.when(level < half - 1)
-            def _():
-                copy_s(i).start()
-
             @pl.when(jnp.logical_not(hop) & (i == 0))
             def _():
                 inbox[1] = fout[0]
@@ -329,15 +325,23 @@
             @pl.when(jnp.logical_not(hop) & (i != e))
             def _():
                 nstage[...] = norm_b
-                copy_n(e).start()
-
-            @pl.when(sends_t(i))
-            def _():
-                copy_t(e).start()
 
             return None
 
         lax.fori_loop(0, 2, forward, None)
+
+        @pl.when(s < half - 1)
+        def _():
+            copy_s(0).start()
+            copy_s(1).start()
+
+        @pl.when(hop)
+        def _():
+            copy_t(e).start()
+
+        @pl.when(jnp.logical_not(hop))
+        def _():
+            copy_n(e).start()
 
         @pl.when(jnp.logical_not(top_line) & (line == line_len - 1))
         def _():
@@ -503,10 +507,6 @@
             def _():
                 copy_g().start()
 
-            @pl.when(level > half)
-            def _():
-                copy_d(i).start()
-
             @pl.when(i == 0)
             def _():
                 gin[1] = gout[0]
@@ -514,6 +514,14 @@
             return None
 
         lax.fori_loop(0, 2, backward, None)
+
+        @pl.when(s >= half)
+        def _():
+            copy_d(0).start()
+
+        @pl.when(s >= half + 2)
+        def _():
+            copy_d(1).start()
 
         @pl.when(pair > 0)
         def _():

time: 163 us -> 159 us (0.975)
  Pallas kernels: 161 us -> 157 us
    pallas_call x1, Pallas kernels: 161 us -> 157 us  [on_device(): pl.pallas_call(make_kernel(sections, replicas, chans, share, scale, PAIR_...]
where the time goes in v5:
time: 159 us
  Pallas kernels  157 us (99%)
  local copies, waits for them, and re-layouts  2.16 us (1%)
    pallas_call x1, Pallas kernels, on_device(): pl.pallas_call(make_kernel(sections, replicas, chans, share, scale, PAIR_...  157 us

profile of v5, /device:TPU:1, one launch (start us, length us, event | category | flops | bytes accessed | tf_op | source)
XLA Modules:
  0.0 159.3 jit_solution(9601323637691381991)
XLA Ops:
  0.0 157.1 %levels.1 = f32[9,40,640]{2,1,0:T(8,128)} custom-call(s32[1,2]{1,0:T(1,128)} %bitcast.11, bf16[2,64,640]{2,1,0:T(8,128)(2,1)} %bitcast.9, bf16[2,64,640]{2,1,0:T(8,128)(2,1)} %bitcast.10, bf16[5760,640]{1,0:T(8,128)(2,1)} %bitcast.7, f32[1000,640]{1,0:T(8,128)} %table_hbm.1), custom_call_target="tpu_custom_call" | custom-call | tf_op jit(solution)/shard_map/levels/pallas_call | solution.py:653
  157.2 2.2 %copy.7 = f32[1,3,3,640,40]{3,4,2,1,0:T(8,128)} copy(f32[1,3,3,640,40]{3,4,2,1,0:T(8,128)} %bitcast.8) | data formatting | bytes 1843200

commit v6 on v5

--- a/solution.py
+++ b/solution.py
@@ -185,7 +185,7 @@
         def spread_z():
             for k in range(2):
                 wait_z(k)
-                for n in (1, xs - 1, 2):
+                for n in (2, 1, xs - 1):
                     copy_v(n, k, x).start()
 
         def spread_x():
@@ -223,13 +223,16 @@
         load_t.wait()
         load_i.wait()
 
+        @pl.when(s >= pair_from)
+        def _():
+            spread_z()
+
         @pl.when(s >= line_len)
         def _():
             turn_weights(e)
 
         @pl.when(s >= pair_from)
         def _():
-            spread_z()
             spread_x()
             spread_y()
 

time: 159 us -> 161 us (1.013)
  Pallas kernels: 157 us -> 159 us
    pallas_call x1, Pallas kernels: 157 us -> 159 us  [on_device(): pl.pallas_call(make_kernel(sections, replicas, chans, share, scale, PAIR_...]
where the time goes in v6:
time: 161 us
  Pallas kernels  159 us (99%)
  local copies, waits for them, and re-layouts  2.16 us (1%)
    pallas_call x1, Pallas kernels, on_device(): pl.pallas_call(make_kernel(sections, replicas, chans, share, scale, PAIR_...  159 us

profile of v6, /device:TPU:1, one launch (start us, length us, event | category | flops | bytes accessed | tf_op | source)
XLA Modules:
  0.0 161.2 jit_solution(16175970792682879109)
XLA Ops:
  0.0 159.1 %levels.1 = f32[9,40,640]{2,1,0:T(8,128)} custom-call(s32[1,2]{1,0:T(1,128)} %bitcast.11, bf16[2,64,640]{2,1,0:T(8,128)(2,1)} %bitcast.9, bf16[2,64,640]{2,1,0:T(8,128)(2,1)} %bitcast.10, bf16[5760,640]{1,0:T(8,128)(2,1)} %bitcast.7, f32[1000,640]{1,0:T(8,128)} %table_hbm.1), custom_call_target="tpu_custom_call" | custom-call | tf_op jit(solution)/shard_map/levels/pallas_call | solution.py:656
  159.1 2.2 %copy.7 = f32[1,3,3,640,40]{3,4,2,1,0:T(8,128)} copy(f32[1,3,3,640,40]{3,4,2,1,0:T(8,128)} %bitcast.8) | data formatting | bytes 1843200
